TPU v7x, 256 devices: a whole 4x4x8 slice. The times are simulated.
256 devices in a mesh: dp: 16 (over y, x_lo, core), head: 16 (over x_hi, z).
Axes of the slice: x: 4 (x_hi: 2, x_lo: 2; x = x_hi * 2 + x_lo), y: 4, z: 8, core: 2. Of those that a mesh axis runs over, the one named last changes fastest.
Arguments:
- latent: bfloat16 [16, 512, 3072], P('dp', None, 'head'), may hold values from -6 to 6
- noise: bfloat16 [16, 512, 3072], P('dp'), may hold values from -18 to 18
- steps: int32 [16], P('dp'), may hold values from 0 to 999
- gen_qkv: bfloat16 [3072, 6144], P(None, 'head'), may hold values from -0.109375 to 0.109375
- gen_out: bfloat16 [2048, 3072], P('head'), may hold values from -0.5 to 0.5
- real_qkv: bfloat16 [3072, 6144], P(None, 'head'), may hold values from -0.109375 to 0.109375
- real_out: bfloat16 [2048, 3072], P('head'), may hold values from -0.5 to 0.5
- fake_qkv: bfloat16 [3072, 6144], P('dp', 'head'), may hold values from -0.109375 to 0.109375
- fake_out: bfloat16 [3072, 2048], P('dp', 'head'), may hold values from -0.5 to 0.5
Outputs:
- score_grad: float32 [16, 512, 3072], P('dp', None, 'head')
- fake_qkv_grad: float32 [3072, 6144], P('dp', 'head')
- fake_out_grad: float32 [3072, 2048], P('dp', 'head')
All inputs are finite; a program needn't handle non-finite values. Where the computation divides by a largest or mean magnitude, that divisor is 1e-20 or more.
Results may differ from a plain program's by a relative error of at most 0.034.
Values may be sent and summed in bfloat16 or wider, within the bound.
No kernel may reach another device: no remote copies, remote signals or barrier semaphores. Data moves between devices by JAX's collectives and lax.ppermute only.
A program may use at most 128 MiB of HBM per device.

v0:
```python
import math

import jax
import jax.numpy as jnp
from jax import lax
from jax.sharding import PartitionSpec as P

D = 3072
HD = 128


highest = lax.Precision.HIGHEST


def layer_norm(values):
    floats = values.astype(jnp.float32)
    center = floats - jnp.mean(floats, axis=-1, keepdims=True)
    spread = jnp.mean(center * center, axis=-1, keepdims=True)
    return (center * lax.rsqrt(spread + 1e-06)).astype(jnp.bfloat16)


def noise_levels(step):
    angle = (step.astype(jnp.float32) + 1.0) / 1001.0 * (math.pi / 2.0)
    return (jnp.cos(angle), jnp.sin(angle))


def attend(packed):
    length = packed.shape[0]
    groups = packed.shape[1] // (3 * HD)
    split = packed.reshape(length, groups, 3, HD)
    query = split[:, :, 0]
    keys = split[:, :, 1]
    values = split[:, :, 2]
    scores = jnp.einsum(
        "qge,kge->gqk", query, keys, preferred_element_type=jnp.float32
    ) / math.sqrt(HD)
    weights = jax.nn.softmax(scores, axis=-1)
    rounded = weights.astype(jnp.bfloat16)
    mixed = jnp.einsum("gqk,kge->qge", rounded, values, preferred_element_type=jnp.float32)
    mixed = mixed.astype(jnp.bfloat16).reshape(length, groups * HD)
    return (weights, rounded, query, keys, values, mixed)


def attend_back(weights, rounded, query, keys, values, grad_mixed):
    length = grad_mixed.shape[0]
    groups = grad_mixed.shape[1] // HD
    upstream = grad_mixed.reshape(length, groups, HD)
    query_f = query.astype(jnp.float32)
    keys_f = keys.astype(jnp.float32)
    values_f = values.astype(jnp.float32)
    grad_values = jnp.einsum(
        "gqk,qge->kge", rounded.astype(jnp.float32), upstream, precision=highest
    )
    grad_weights = jnp.einsum("qge,kge->gqk", upstream, values_f, precision=highest)
    inner = jnp.sum(grad_weights * weights, axis=-1, keepdims=True)
    grad_scores = weights * (grad_weights - inner) / math.sqrt(HD)
    grad_query = jnp.einsum("gqk,kge->qge", grad_scores, keys_f, precision=highest)
    grad_keys = jnp.einsum("gqk,qge->kge", grad_scores, query_f, precision=highest)
    stacked = jnp.stack([grad_query, grad_keys, grad_values], axis=2)
    return stacked.reshape(length, groups * 3 * HD).astype(jnp.bfloat16)


def local(latent, noise, steps, gen_qkv, gen_out, real_qkv, real_out, fake_qkv, fake_out):
    tokens_shard = latent[0]
    fresh = noise[0]
    length = tokens_shard.shape[0]
    width_shard = tokens_shard.shape[1]
    position = lax.axis_index("head")
    fresh_cols = lax.dynamic_slice_in_dim(fresh, position * width_shard, width_shard, 1)
    signal_scale, noise_scale = noise_levels(steps[0])
    inv_root = 1.0 / math.sqrt(length * lax.axis_size("dp"))
    whole = lax.all_gather(tokens_shard, "head", axis=1, tiled=True)
    gen_packed = jnp.dot(layer_norm(whole), gen_qkv, preferred_element_type=jnp.float32).astype(
        jnp.bfloat16
    )
    gen_mixed = attend(gen_packed)[5]
    gen_terms = jnp.dot(gen_mixed, gen_out, preferred_element_type=jnp.float32)
    branch = lax.psum_scatter(
        gen_terms.astype(jnp.bfloat16), "head", scatter_dimension=1, tiled=True
    ).astype(jnp.float32)
    generated = (tokens_shard.astype(jnp.float32) + branch).astype(jnp.bfloat16)
    noised_part = (
        signal_scale * generated.astype(jnp.float32) + noise_scale * fresh_cols.astype(jnp.float32)
    ).astype(jnp.bfloat16)
    noised = lax.all_gather(noised_part, "head", axis=1, tiled=True)
    normed = layer_norm(noised)
    real_packed = jnp.dot(normed, real_qkv, preferred_element_type=jnp.float32).astype(jnp.bfloat16)
    real_terms = jnp.dot(attend(real_packed)[5], real_out, preferred_element_type=jnp.float32)
    columns = normed
    fake_packed = jnp.dot(
        columns,
        lax.all_gather(fake_qkv, "dp", axis=0, tiled=True),
        preferred_element_type=jnp.float32,
    ).astype(jnp.bfloat16)
    weights, rounded, query, keys, values, fake_mixed = attend(fake_packed)
    fake_terms = lax.dot_general(
        fake_mixed,
        lax.all_gather(fake_out, "dp", axis=0, tiled=True),
        (((1,), (1,)), ((), ())),
        preferred_element_type=jnp.float32,
    )
    real_eps, fake_eps = (
        lax.psum_scatter(
            real_terms.astype(jnp.bfloat16), "head", scatter_dimension=1, tiled=True
        ).astype(jnp.float32),
        lax.psum_scatter(
            fake_terms.astype(jnp.bfloat16), "head", scatter_dimension=1, tiled=True
        ).astype(jnp.float32),
    )
    error_part = ((fake_eps - fresh_cols.astype(jnp.float32)) * inv_root).astype(jnp.bfloat16)
    error = lax.all_gather(error_part, "head", axis=1, tiled=True)
    gap_local = jnp.sum(jnp.abs(fresh_cols.astype(jnp.float32) - real_eps))
    gap = lax.psum(gap_local, "head") / (length * D)
    score_grad = ((real_eps - fake_eps) / (gap + 1e-05))[None]
    out_rows = lax.all_gather(fake_out, "dp", axis=0, tiled=True)
    grad_mixed = jnp.dot(error, out_rows, preferred_element_type=jnp.float32)
    grad_packed = attend_back(weights, rounded, query, keys, values, grad_mixed)
    columns = normed
    fake_qkv_grad = lax.psum_scatter(
        lax.dot_general(
            columns, grad_packed, (((0,), (0,)), ((), ())), preferred_element_type=jnp.float32
        ).astype(jnp.bfloat16),
        "dp",
        scatter_dimension=0,
        tiled=True,
    ).astype(jnp.float32)
    columns = error
    fake_out_grad = lax.psum_scatter(
        lax.dot_general(
            columns, fake_mixed, (((0,), (0,)), ((), ())), preferred_element_type=jnp.float32
        ).astype(jnp.bfloat16),
        "dp",
        scatter_dimension=0,
        tiled=True,
    ).astype(jnp.float32)
    return (score_grad, fake_qkv_grad, fake_out_grad)


def solution(mesh):
    in_specs = (
        P("dp", None, "head"),
        P("dp", None, None),
        P("dp"),
        P(None, "head"),
        P("head", None),
        P(None, "head"),
        P("head", None),
        P("dp", "head"),
        P("dp", "head"),
    )
    out_specs = (P("dp", None, "head"), P("dp", "head"), P("dp", "head"))
    return jax.shard_map(local, mesh=mesh, in_specs=in_specs, out_specs=out_specs, check_vma=False)
```

profile of v0, /device:TPU:4, one launch (start us, length us, event | category | flops | bytes accessed | tf_op | source)
XLA Modules:
  0.0 1118.9 jit_solution(150016499548865358)
XLA Ops:
  8.0 96.5 %all-gather.12.cloned.1.call-done = bf16[1,512,3072]{1,2,0:T(8,128)(2,1)} async-done(((bf16[1,512,192]{1,2,0:T(8,128)(2,1)}), bf16[1,512,3072]{1,2,0:T(8,128)(2,1)}) %all-gather.12.cloned.1.call-update) | async-done | bytes 3145744 | tf_op jit(solution)/shard_map/all_gather | solution.py:72
  104.5 2.5 convert_reduce_fusion
  107.3 0.9 fusion.7
  108.2 1.5 fusion.24
  110.0 1.0 copy-done.7
  111.2 4.4 convolution_convert_fusion.2
  117.4 1.1 copy.13
  118.5 204.8 %reduce-scatter.6.cloned.1.call-done = bf16[512,192]{0,1:T(8,128)(2,1)} async-done(((bf16[512,3072]{0,1:T(8,128)(2,1)}), bf16[512,192]{0,1:T(8,128)(2,1)}) %reduce-scatter.6.cloned.1.call-update) | async-done | bytes 196624 | tf_op jit(solution)/shard_map/reduce_scatter | solution.py:78
  323.2 1.7 fusion.48
  325.6 91.6 %all-gather.6.cloned.1.call-done = bf16[512,3072]{0,1:T(8,128)(2,1)} async-done(((bf16[512,192]{0,1:T(8,128)(2,1)}), bf16[512,3072]{0,1:T(8,128)(2,1)}) %all-gather.6.cloned.1.call-update) | async-done | bytes 3145744 | tf_op jit(solution)/shard_map/all_gather | solution.py:85
  417.2 2.5 convert_reduce_fusion.1
  420.0 0.9 fusion.2
  420.9 1.4 fusion.18
  423.5 1.1 copy-done.8
  424.7 4.5 convolution_convert_fusion.1
  429.3 26.5 %all_gather.19 = bf16[3072,128]{1,0:T(8,128)(2,1)} all-gather(bf16[192,128]{1,0:T(8,128)(2,1)S(1)} %copy-done.15), channel_id=1, replica_groups=mesh['dp'=16,'head'=16] {'dp'}, dimensions={0}, use_global_device_ids=true | all-gather | bytes 835584 | tf_op jit(solution)/shard_map/all_gather | solution.py:98
  456.3 4.1 fusion.21
  462.1 2.7 convolution_convert_fusion
  464.9 204.8 %reduce-scatter.8.cloned.1.call-done = bf16[512,192]{0,1:T(8,128)(2,1)} async-done(((bf16[512,3072]{0,1:T(8,128)(2,1)}), bf16[512,192]{0,1:T(8,128)(2,1)}) %reduce-scatter.8.cloned.1.call-update) | async-done | bytes 196624 | tf_op jit(solution)/shard_map/reduce_scatter | solution.py:103
  669.7 211.7 %reduce-scatter.10.cloned.1.call-done = bf16[512,192]{0,1:T(8,128)(2,1)} async-done(((bf16[512,3072]{0,1:T(8,128)(2,1)}), bf16[512,192]{0,1:T(8,128)(2,1)}) %reduce-scatter.10.cloned.1.call-update) | async-done | bytes 196624 | tf_op jit(solution)/shard_map/reduce_scatter | solution.py:106
  881.4 2.4 fusion.52
  883.9 91.4 %all-gather.10.cloned.1.call-done = bf16[512,3072]{0,1:T(8,128)(2,1)} async-done(((bf16[512,192]{0,1:T(8,128)(2,1)}), bf16[512,3072]{0,1:T(8,128)(2,1)}) %all-gather.10.cloned.1.call-update) | async-done | bytes 3145744 | tf_op jit(solution)/shard_map/all_gather | solution.py:111
  975.4 3.8 convolution_convert_fusion.4
  979.2 3.2 fusion.66
  984.7 1.0 fusion.32
  985.7 0.9 copy-done.2
  986.6 3.3 convolution_convert_fusion.3
  989.9 41.3 %psum.7 = f32[]{:T(128)} all-reduce(f32[]{:T(128)} %get-tuple-element.4), channel_id=1, replica_groups=mesh['dp'=16,'head'=16] {'head'}, use_global_device_ids=true, to_apply=%region_14.0 | all-reduce | flops 1 | bytes 8 | tf_op jit(solution)/shard_map/psum | solution.py:113
  1032.7 9.8 reduce-scatter.14.cloned.1.call-done
  1042.5 1.4 convert_element_type.162
  1043.9 66.8 %reduce-scatter.12.cloned.1.call-done = bf16[192,384]{1,0:T(8,128)(2,1)} async-done(((bf16[3072,384]{1,0:T(8,128)(2,1)}), bf16[192,384]{1,0:T(8,128)(2,1)}) %reduce-scatter.12.cloned.1.call-update) | async-done | bytes 147472 | tf_op jit(solution)/shard_map/reduce_scatter | solution.py:119
  1110.8 1.6 convert_element_type.160
  (69 shorter events, 10.4 us)
Async XLA Ops:
  7.2 109.4 %copy-start = (bf16[1,512,3072]{2,1,0:T(8,128)(2,1)S(1)}, bf16[1,512,3072]{2,1,0:T(8,128)(2,1)}, u32[]{:S(2)}) copy-start(bf16[1,512,3072]{2,1,0:T(8,128)(2,1)} %param.10) | copy-start | bytes 9437188
  7.2 97.3 %all-gather.12.cloned.1.call-start = ((), (), s32[]{:S(2)}) async-start(), calls=%async_computation.13 | async-start | bytes 3342336 | tf_op jit(solution)/shard_map/all_gather | solution.py:72
  7.9 315.3 %reduce-scatter.6.cloned.1.call-start = ((), (), s32[]{:S(2)}) async-start(), calls=%async_computation.5 | async-start | bytes 3342336 | tf_op jit(solution)/shard_map/reduce_scatter | solution.py:78
  104.5 2.8 copy-start.3
  104.5 3.7 copy-start.16
  110.0 1.0 copy-start.7
  115.6 207.6 %copy-start.9 = (bf16[1,512,192]{1,2,0:T(8,128)(2,1)S(1)}, bf16[1,512,192]{1,2,0:T(8,128)(2,1)}, u32[]{:S(2)}) copy-start(bf16[1,512,192]{1,2,0:T(8,128)(2,1)} %param.9) | copy-start | bytes 589828
  115.6 301.5 %all-gather.6.cloned.1.call-start = ((), (), s32[]{:S(2)}) async-start(), calls=%async_computation.6 | async-start | bytes 3342336 | tf_op jit(solution)/shard_map/all_gather | solution.py:85
  325.0 131.4 %all-gather.8.cloned.1.call-start = ((), (), s32[]{:S(2)}) async-start(), calls=%async_computation.8 | async-start | bytes 2506752 | tf_op jit(solution)/shard_map/all_gather | solution.py:92
  325.5 344.2 %reduce-scatter.8.cloned.1.call-start = ((), (), s32[]{:S(2)}) async-start(), calls=%async_computation.7 | async-start | bytes 3342336 | tf_op jit(solution)/shard_map/reduce_scatter | solution.py:103
  417.2 2.8 copy-start.1
  417.2 3.7 copy-start.17
  422.4 0.7 copy-start.14
  423.5 1.1 copy-start.8
  424.7 4.6 copy-start.15
  429.2 452.2 %reduce-scatter.10.cloned.1.call-start = ((), (), s32[]{:S(2)}) async-start(), calls=%async_computation.9 | async-start | bytes 3342336 | tf_op jit(solution)/shard_map/reduce_scatter | solution.py:106
  460.4 1.7 copy-start.12
  460.4 1.7 copy-start.4
  460.8 1.0 copy-start.5
  464.8 510.5 %all-gather.10.cloned.1.call-start = ((), (), s32[]{:S(2)}) async-start(), calls=%async_computation.10 | async-start | bytes 3342336 | tf_op jit(solution)/shard_map/all_gather | solution.py:111
  883.9 158.6 %reduce-scatter.14.cloned.1.call-start = ((), (), s32[]{:S(2)}) async-start(), calls=%async_computation.12 | async-start | bytes 835584 | tf_op jit(solution)/shard_map/reduce_scatter | solution.py:128
  979.1 4.0 copy-start.13
  979.1 131.6 %reduce-scatter.12.cloned.1.call-start = ((), (), s32[]{:S(2)}) async-start(), calls=%async_computation.11 | async-start | bytes 2506752 | tf_op jit(solution)/shard_map/reduce_scatter | solution.py:119
  979.2 3.2 copy-start.6
  984.7 1.9 copy-start.2
  986.6 45.3 %copy-start.10 = (bf16[512,192]{0,1:T(8,128)(2,1)S(1)}, bf16[512,192]{0,1:T(8,128)(2,1)}, u32[]{:S(2)}) copy-start(bf16[512,192]{0,1:T(8,128)(2,1)} %reduce-scatter.8.cloned.1.call-done) | copy-start | bytes 589828
  986.6 45.3 %copy-start.11 = (bf16[512,192]{0,1:T(8,128)(2,1)S(1)}, bf16[512,192]{0,1:T(8,128)(2,1)}, u32[]{:S(2)}) copy-start(bf16[512,192]{0,1:T(8,128)(2,1)} %reduce-scatter.10.cloned.1.call-done) | copy-start | bytes 589828
Sparse Core Ops, SparseCore 0:
  10.6 93.8 all-gather.11
  115.8 207.4 reduce-scatter.5
  326.7 90.3 all-gather.5
  419.0 37.2 all-gather.7
  460.7 208.9 reduce-scatter.7
  673.5 207.8 reduce-scatter.9
  884.9 90.3 all-gather.9
  979.2 63.1 reduce-scatter.13
  1045.0 65.6 reduce-scatter.11
where the time goes:
time: 1120 us
  waiting for transfers between devices  979 us (87%)
  blocking collectives  67.8 us (6%)
  matrix products  33.3 us (3%)
  between operations  15.6 us (1%)
  other arithmetic  15.5 us (1%)
    reduce_scatter x1, waiting for transfers between devices, local(): lax.psum_scatter(fake_terms.astype(jnp.bfloat16), 'head', scatter_dimensi...  212 us
    reduce_scatter x1, waiting for transfers between devices, local(): lax.psum_scatter(real_terms.astype(jnp.bfloat16), 'head', scatter_dimensi...  205 us
    reduce_scatter x1, waiting for transfers between devices, local(): lax.psum_scatter(gen_terms.astype(jnp.bfloat16), 'head', scatter_dimensio...  205 us
    all_gather x1, waiting for transfers between devices, local(): whole = lax.all_gather(tokens_shard, 'head', axis=1, tiled=True)  96.5 us
    all_gather x1, waiting for transfers between devices, local(): noised = lax.all_gather(noised_part, 'head', axis=1, tiled=True)  91.6 us
    all_gather x1, waiting for transfers between devices, local(): error = lax.all_gather(error_part, 'head', axis=1, tiled=True)  91.4 us
    reduce_scatter x1, waiting for transfers between devices, local(): lax.psum_scatter(lax.dot_general(columns, grad_packed, (((0,), (0,)), (()...  66.8 us
    psum x1, blocking collectives, local(): gap = lax.psum(gap_local, 'head') / (length * D)  41.3 us
  transfers between devices with their start and end apart: 9, of which 9 were waited for; matrix products, arithmetic and copies ran while one was open for 3% of the time, Pallas kernels for 0%

commit v1 on v0

v1 whole, which is shorter than its diff:
```python
import math

import jax
import jax.numpy as jnp
from jax import lax
from jax.sharding import PartitionSpec as P

D = 3072
HD = 128
F = 192
BF = jnp.bfloat16
F32 = jnp.float32


def gather_head(block):
    return lax.all_gather(block, "head", axis=0, tiled=True)


def spread(block, axis):
    return lax.all_to_all(jnp.broadcast_to(block[None], (16,) + block.shape), axis, 0, 0)


def collect(parts, axis):
    got = lax.all_to_all(parts, axis, 0, 0)
    return jnp.sum(got.astype(F32), axis=0)


def layer_norm(values):
    floats = values.astype(F32)
    center = floats - jnp.mean(floats, axis=0, keepdims=True)
    spread = jnp.mean(center * center, axis=0, keepdims=True)
    return (center * lax.rsqrt(spread + 1e-06)).astype(BF)


def noise_levels(step):
    angle = (step.astype(F32) + 1.0) / 1001.0 * (math.pi / 2.0)
    return (jnp.cos(angle), jnp.sin(angle))


def dot(a, b, ca, cb):
    return lax.dot_general(a, b, (((ca,), (cb,)), ((), ())), preferred_element_type=F32)


def attend(packed):
    query, keys, values = packed[:, :HD], packed[:, HD : 2 * HD], packed[:, 2 * HD :]
    scores = dot(query, keys, 1, 1) / math.sqrt(HD)
    weights = jax.nn.softmax(scores, axis=-1)
    rounded = weights.astype(BF)
    mixed = dot(values, rounded, 0, 1).astype(BF)
    return weights, rounded, query, keys, values, mixed


def attend_back(weights, rounded, query, keys, values, grad_mixed):
    upstream = grad_mixed.astype(BF)
    grad_values = dot(rounded, upstream, 0, 0)
    grad_weights = dot(upstream, values, 1, 1)
    inner = jnp.sum(grad_weights * weights, axis=-1, keepdims=True)
    grad_scores = (weights * (grad_weights - inner) / math.sqrt(HD)).astype(BF)
    grad_query = dot(grad_scores, keys, 1, 0)
    grad_keys = dot(grad_scores, query, 0, 0)
    return jnp.concatenate([grad_query, grad_keys, grad_values], axis=1).astype(BF)


def local(latent, noise, steps, gen_qkv, gen_out, real_qkv, real_out, fake_qkv, fake_out):
    fresh = noise[0]
    length = fresh.shape[0]
    head = lax.axis_index("head")
    signal_scale, noise_scale = noise_levels(steps[0])
    inv_root = 1.0 / math.sqrt(length * lax.axis_size("dp"))
    fresh_cols = lax.dynamic_slice_in_dim(fresh, head * F, F, 1).T.astype(F32)

    def out_chunk(w):
        got = lax.all_to_all(w.reshape(16, F, HD), "head", 0, 0)
        return got.transpose(1, 0, 2).reshape(F, 16 * HD)

    tokens = latent[0].T
    whole = gather_head(tokens)
    gen_chunk = out_chunk(gen_out.T)
    fake_both = spread(jnp.concatenate([fake_qkv, fake_out], axis=1), "dp").reshape(D, 4 * HD)
    fake_full, fake_cols = fake_both[:, : 3 * HD], fake_both[:, 3 * HD :]
    fake_rows = spread(fake_out, "head").transpose(1, 0, 2).reshape(F, 16 * HD)
    fake_chunk = out_chunk(fake_cols)
    real_chunk = out_chunk(real_out.T)
    gram = collect(dot(fake_rows, fake_out, 0, 0).astype(BF).reshape(16, HD, HD), "dp")
    gram = spread(gram.astype(BF), "dp").reshape(16 * HD, HD)
    noise_back = dot(fresh, fake_cols, 1, 0)

    gen_packed = dot(layer_norm(whole), gen_qkv, 0, 0).astype(BF)
    gen_mixed = gather_head(attend(gen_packed)[5])
    branch = dot(gen_chunk, gen_mixed, 1, 0)
    generated = (tokens.astype(F32) + branch).astype(BF)
    noised_part = (signal_scale * generated.astype(F32) + noise_scale * fresh_cols).astype(BF)
    normed = layer_norm(gather_head(noised_part))

    fake_packed = dot(normed, fake_full, 0, 0).astype(BF)
    weights, rounded, query, keys, values, fake_mixed = attend(fake_packed)
    fake_all = gather_head(fake_mixed)
    real_packed = dot(normed, real_qkv, 0, 0).astype(BF)
    real_all = gather_head(attend(real_packed)[5])

    grad_mixed = inv_root * (dot(fake_all, gram, 0, 0) - noise_back)
    grad_packed = attend_back(weights, rounded, query, keys, values, grad_mixed)
    qkv_grad = dot(normed, grad_packed, 1, 0).astype(BF)
    fake_qkv_grad = collect(qkv_grad.reshape(16, F, 3 * HD), "dp")

    noise_term = dot(fresh, fake_mixed, 0, 1).astype(BF).reshape(16, F, HD)
    square = dot(fake_all, fake_mixed, 1, 1).astype(BF).reshape(16, HD, HD)
    summed = collect(jnp.concatenate([noise_term, square], axis=1), "dp")
    square_all = spread(summed[F:].astype(BF), "dp").reshape(16 * HD, HD)
    fake_out_grad = inv_root * (dot(fake_rows, square_all, 1, 0) - summed[:F])

    fake_eps = dot(fake_chunk, fake_all, 1, 0)
    real_eps = dot(real_chunk, real_all, 1, 0)
    gap_part = jnp.sum(jnp.abs(fresh_cols - real_eps))
    gap = jnp.sum(spread(jnp.full((1, HD), gap_part, F32), "head")[:, 0, 0]) / (length * D)
    score_grad = ((real_eps - fake_eps) / (gap + 1e-05)).T[None]
    return (score_grad, fake_qkv_grad, fake_out_grad)


def solution(mesh):
    in_specs = (
        P("dp", None, "head"),
        P("dp", None, None),
        P("dp"),
        P(None, "head"),
        P("head", None),
        P(None, "head"),
        P("head", None),
        P("dp", "head"),
        P("dp", "head"),
    )
    out_specs = (P("dp", None, "head"), P("dp", "head"), P("dp", "head"))
    return jax.shard_map(local, mesh=mesh, in_specs=in_specs, out_specs=out_specs, check_vma=False)
```

time: 1120 us -> 566 us (0.51)
  waiting for transfers between devices: 979 us -> 393 us
  blocking collectives: 67.8 us -> 0 us
  starting transfers between devices: 0.37 us -> 67.9 us
  matrix products: 33.3 us -> 49 us
  local copies, waits for them, and re-layouts: 7.01 us -> 20.5 us
    reduce_scatter x5 -> x0, waiting for transfers between devices: 698 us -> none  [the longest x1 212 us: local(): lax.psum_scatter(fake_terms.astype(jnp.bfloat16), 'head', scatter_dimensi...]
    all_to_all x0 -> x11, waiting for transfers between devices: none -> 110 us  [the longest x3 45 us: out_chunk(): got = lax.all_to_all(w.reshape(16, F, HD), 'head', 0, 0)]
    all_to_all x0 -> x11, starting transfers between devices: none -> 67.7 us  [the longest x5 30.2 us: spread(): lax.all_to_all(jnp.broadcast_to(block[None], (16,) + block.shape), axis,...]
    psum x1 -> x0, blocking collectives: 41.3 us -> none  [local(): gap = lax.psum(gap_local, 'head') / (length * D)]
    all_gather x1 -> x0, blocking collectives: 26.5 us -> none  [local(): lax.all_gather(fake_out, 'dp', axis=0, tiled=True)]
    dot_general x17 -> x23, matrix products: 33.3 us -> 49 us  [dot(): lax.dot_general(a, b, (((ca,), (cb,)), ((), ())), preferred_element_type=...]
    all_gather x4 -> x5, waiting for transfers between devices: 280 us -> 283 us  [gather_head(): return lax.all_gather(block, 'head', axis=0, tiled=True)]
  transfers between devices with their start and end apart: 9 -> 16, of which waited for: 9 -> 13; matrix products, arithmetic and copies ran while one was open for 3% -> 11% of each run, Pallas kernels for 0% -> 0%
where the time goes in v1:
time: 566 us; the launch traced here: 562 us
  waiting for transfers between devices  393 us (69%)
  starting transfers between devices  67.9 us (12%)
  matrix products  49 us (9%)
  local copies, waits for them, and re-layouts  20.5 us (4%)
  other arithmetic  16 us (3%)
  between operations  15.5 us (3%)
    all_gather x5, waiting for transfers between devices, gather_head(): return lax.all_gather(block, 'head', axis=0, tiled=True)  283 us
    dot_general x23, matrix products, dot(): lax.dot_general(a, b, (((ca,), (cb,)), ((), ())), preferred_element_type=...  49 us
    all_to_all x3, waiting for transfers between devices, out_chunk(): got = lax.all_to_all(w.reshape(16, F, HD), 'head', 0, 0)  45 us
    all_to_all x5, waiting for transfers between devices, spread(): lax.all_to_all(jnp.broadcast_to(block[None], (16,) + block.shape), axis,...  34.6 us
    all_to_all x3, waiting for transfers between devices, collect(): got = lax.all_to_all(parts, axis, 0, 0)  30.4 us
    all_to_all x5, starting transfers between devices, spread(): lax.all_to_all(jnp.broadcast_to(block[None], (16,) + block.shape), axis,...  30.2 us
    all_to_all x3, starting transfers between devices, out_chunk(): got = lax.all_to_all(w.reshape(16, F, HD), 'head', 0, 0)  22.6 us
    all_to_all x3, starting transfers between devices, collect(): got = lax.all_to_all(parts, axis, 0, 0)  15 us
  transfers between devices with their start and end apart: 16, of which 13 were waited for; matrix products, arithmetic and copies ran while one was open for 11% of the time, Pallas kernels for 0%

profile of v1, /device:TPU:4, one launch (start us, length us, event | category | flops | bytes accessed | tf_op | source)
XLA Modules:
  0.0 562.4 jit_solution(10586546725822228637)
XLA Ops:
  8.0 96.5 %all-gather.6.cloned.1.call-done = bf16[3072,512]{1,0:T(8,128)(2,1)} async-done(((bf16[192,512]{1,0:T(8,128)(2,1)}), bf16[3072,512]{1,0:T(8,128)(2,1)}) %all-gather.6.cloned.1.call-update) | async-done | bytes 3145744 | tf_op jit(solution)/shard_map/all_gather | solution.py:16
  113.9 7.2 %all-to-all-start = ((bf16[16,192,128]{2,1,0:T(8,128)(2,1)}), bf16[16,192,128]{2,1,0:T(8,128)(2,1)}, u32[]{:S(2)}, u32[]{:S(2)}) async-start(bf16[16,192,128]{2,1,0:T(8,128)(2,1)} %bitcast.115), calls=%async_computation | async-start | bytes 1572864 | tf_op jit(solution)/shard_map/all_to_all | solution.py:73
  123.0 17.9 %all-to-all-done = bf16[16,192,128]{2,1,0:T(8,128)(2,1)} async-done(((bf16[16,192,128]{2,1,0:T(8,128)(2,1)}), bf16[16,192,128]{2,1,0:T(8,128)(2,1)}, u32[]{:S(2)}, u32[]{:S(2)}) %all-to-all-start) | async-done | bytes 786464 | tf_op jit(solution)/shard_map/all_to_all | solution.py:73
  140.9 56.2 %all-gather.8.cloned.1.call-done = bf16[2048,512]{1,0:T(8,128)(2,1)} async-done(((bf16[128,512]{1,0:T(8,128)(2,1)}), bf16[2048,512]{1,0:T(8,128)(2,1)}) %all-gather.8.cloned.1.call-update) | async-done | bytes 2097168 | tf_op jit(solution)/shard_map/all_gather | solution.py:16
  197.0 3.1 fusion.40
  202.3 5.8 %all-to-all-start.2 = ((bf16[16,192,512]{2,1,0:T(8,128)(2,1)}), bf16[16,192,512]{2,1,0:T(8,128)(2,1)}, u32[]{:S(2)}, u32[]{:S(2)}) async-start(bf16[16,192,512]{2,1,0:T(8,128)(2,1)} %broadcast_in_dim.10), calls=%async_computation.2 | async-start | bytes 6291456 | tf_op jit(solution)/shard_map/all_to_all | solution.py:20
  208.1 82.2 %all-gather.10.cloned.1.call-done = bf16[3072,512]{1,0:T(8,128)(2,1)} async-done(((bf16[192,512]{1,0:T(8,128)(2,1)}), bf16[3072,512]{1,0:T(8,128)(2,1)}) %all-gather.10.cloned.1.call-update) | async-done | bytes 3145744 | tf_op jit(solution)/shard_map/all_gather | solution.py:16
  294.0 4.5 fusion.28
  301.9 7.1 %all-to-all-start.5 = ((bf16[16,192,128]{2,1,0:T(8,128)(2,1)}), bf16[16,192,128]{2,1,0:T(8,128)(2,1)}, u32[]{:S(2)}, u32[]{:S(2)}) async-start(bf16[16,192,128]{2,1,0:T(8,128)(2,1)} %broadcast_in_dim.12), calls=%async_computation.5 | async-start | bytes 1572864 | tf_op jit(solution)/shard_map/all_to_all | solution.py:20
  311.4 17.1 %all-to-all-done.5 = bf16[16,192,128]{2,1,0:T(8,128)(2,1)} async-done(((bf16[16,192,128]{2,1,0:T(8,128)(2,1)}), bf16[16,192,128]{2,1,0:T(8,128)(2,1)}, u32[]{:S(2)}, u32[]{:S(2)}) %all-to-all-start.5) | async-done | bytes 786464 | tf_op jit(solution)/shard_map/all_to_all | solution.py:20
  330.9 6.1 %all-to-all-start.6 = ((bf16[16,128,128]{2,1,0:T(8,128)(2,1)}), bf16[16,128,128]{2,1,0:T(8,128)(2,1)}, u32[]{:S(2)}, u32[]{:S(2)}) async-start(bf16[16,128,128]{2,1,0:T(8,128)(2,1)} %bitcast.120), calls=%async_computation.6 | async-start | bytes 1048576 | tf_op jit(solution)/shard_map/all_to_all | solution.py:24
  337.1 4.5 fusion.22
  341.5 6.4 %all-to-all-done.6 = bf16[16,128,128]{2,1,0:T(8,128)(2,1)} async-done(((bf16[16,128,128]{2,1,0:T(8,128)(2,1)}), bf16[16,128,128]{2,1,0:T(8,128)(2,1)}, u32[]{:S(2)}, u32[]{:S(2)}) %all-to-all-start.6) | async-done | bytes 524320 | tf_op jit(solution)/shard_map/all_to_all | solution.py:24
  348.0 7.7 %all-to-all-start.1 = ((bf16[16,192,128]{2,1,0:T(8,128)(2,1)}), bf16[16,192,128]{2,1,0:T(8,128)(2,1)}, u32[]{:S(2)}, u32[]{:S(2)}) async-start(bf16[16,192,128]{2,1,0:T(8,128)(2,1)} %bitcast.114), calls=%async_computation.1 | async-start | bytes 1572864 | tf_op jit(solution)/shard_map/all_to_all | solution.py:73
  358.4 19.2 %all-to-all-done.1 = bf16[16,192,128]{2,1,0:T(8,128)(2,1)} async-done(((bf16[16,192,128]{2,1,0:T(8,128)(2,1)}), bf16[16,192,128]{2,1,0:T(8,128)(2,1)}, u32[]{:S(2)}, u32[]{:S(2)}) %all-to-all-start.1) | async-done | bytes 786464 | tf_op jit(solution)/shard_map/all_to_all | solution.py:73
  378.5 4.2 all-to-all-start.7
  384.8 8.8 %all-to-all-done.7 = bf16[16,128,128]{2,1,0:T(8,128)(2,1)} async-done(((bf16[16,128,128]{2,1,0:T(8,128)(2,1)}), bf16[16,128,128]{2,1,0:T(8,128)(2,1)}, u32[]{:S(2)}, u32[]{:S(2)}) %all-to-all-start.7) | async-done | bytes 524320 | tf_op jit(solution)/shard_map/all_to_all | solution.py:20
  393.6 7.7 %all-to-all-start.3 = ((bf16[16,192,128]{2,1,0:T(8,128)(2,1)}), bf16[16,192,128]{2,1,0:T(8,128)(2,1)}, u32[]{:S(2)}, u32[]{:S(2)}) async-start(bf16[16,192,128]{2,1,0:T(8,128)(2,1)} %bitcast.116), calls=%async_computation.3 | async-start | bytes 1572864 | tf_op jit(solution)/shard_map/all_to_all | solution.py:73
  401.3 2.8 fusion.42
  415.3 7.8 %all-to-all-done.3 = bf16[16,192,128]{2,1,0:T(8,128)(2,1)} async-done(((bf16[16,192,128]{2,1,0:T(8,128)(2,1)}), bf16[16,192,128]{2,1,0:T(8,128)(2,1)}, u32[]{:S(2)}, u32[]{:S(2)}) %all-to-all-start.3) | async-done | bytes 786464 | tf_op jit(solution)/shard_map/all_to_all | solution.py:73
  423.1 4.4 all-to-all-start.9
  432.3 47.9 %all-gather.12.cloned.1.call-done = bf16[2048,512]{1,0:T(8,128)(2,1)} async-done(((bf16[128,512]{1,0:T(8,128)(2,1)}), bf16[2048,512]{1,0:T(8,128)(2,1)}) %all-gather.12.cloned.1.call-update) | async-done | bytes 2097168 | tf_op jit(solution)/shard_map/all_gather | solution.py:16
  480.2 3.7 fusion.64
  485.2 7.1 %all-to-all-start.4 = ((f32[16,1,128]{2,1,0:T(1,128)}), f32[16,1,128]{2,1,0:T(1,128)S(1)}, u32[]{:S(2)}, u32[]{:S(2)}) async-start(f32[16,1,128]{2,1,0:T(1,128)} %broadcast_in_dim_broadcast_in_dim_broadcast_in_dim.3), calls=%async_computation.4 | async-start | bytes 16384 | tf_op jit(solution)/shard_map/all_to_all | solution.py:20
  495.1 4.3 all-to-all-done.4
  501.1 5.9 %all-to-all-start.10 = ((bf16[16,128,128]{2,1,0:T(8,128)(2,1)}), bf16[16,128,128]{2,1,0:T(8,128)(2,1)}, u32[]{:S(2)}, u32[]{:S(2)}) async-start(bf16[16,128,128]{2,1,0:T(8,128)(2,1)} %broadcast_in_dim.14), calls=%async_computation.10 | async-start | bytes 1048576 | tf_op jit(solution)/shard_map/all_to_all | solution.py:20
  508.3 5.2 convolution_convert_fusion
  513.5 4.4 all-to-all-done.10
  518.0 4.4 all-to-all-start.8
  523.7 3.2 fusion.35
  529.2 24.0 %all-to-all-done.8 = bf16[16,192,384]{2,1,0:T(8,128)(2,1)} async-done(((bf16[16,192,384]{2,1,0:T(8,128)(2,1)}), bf16[16,192,384]{2,1,0:T(8,128)(2,1)}, u32[]{:S(2)}, u32[]{:S(2)}) %all-to-all-start.8) | async-done | bytes 2359328 | tf_op jit(solution)/shard_map/all_to_all | solution.py:24
  553.1 2.7 convert_reduce_fusion.2
  (90 shorter events, 56.7 us)
Async XLA Ops:
  7.2 114.8 %copy-start = (bf16[1,512,3072]{2,1,0:T(8,128)(2,1)S(1)}, bf16[1,512,3072]{2,1,0:T(8,128)(2,1)}, u32[]{:S(2)}) copy-start(bf16[1,512,3072]{2,1,0:T(8,128)(2,1)} %param.10) | copy-start | bytes 9437188
  7.2 97.3 %all-gather.6.cloned.1.call-start = ((), (), s32[]{:S(2)}) async-start(), calls=%async_computation.11 | async-start | bytes 3342336 | tf_op jit(solution)/shard_map/all_gather | solution.py:16
  7.9 189.1 %all-gather.8.cloned.1.call-start = ((), (), s32[]{:S(2)}) async-start(), calls=%async_computation.12 | async-start | bytes 2228224 | tf_op jit(solution)/shard_map/all_gather | solution.py:16
  104.5 2.8 copy-start.2
  104.5 3.7 copy-start.15
  113.9 86.3 %copy-start.12 = (bf16[192,128]{1,0:T(8,128)(2,1)S(1)}, bf16[192,128]{1,0:T(8,128)(2,1)}, u32[]{:S(2)}) copy-start(bf16[192,128]{1,0:T(8,128)(2,1)} %param.17) | copy-start | bytes 147460
  113.9 27.0 %all-to-all-start = ((bf16[16,192,128]{2,1,0:T(8,128)(2,1)}), bf16[16,192,128]{2,1,0:T(8,128)(2,1)}, u32[]{:S(2)}, u32[]{:S(2)}) async-start(bf16[16,192,128]{2,1,0:T(8,128)(2,1)} %bitcast.115), calls=%async_computation | async-start | bytes 1572864 | tf_op jit(solution)/shard_map/all_to_all | solution.py:73
  121.1 169.2 %all-gather.10.cloned.1.call-start = ((), (), s32[]{:S(2)}) async-start(), calls=%async_computation.13 | async-start | bytes 3342336 | tf_op jit(solution)/shard_map/all_gather | solution.py:16
  123.0 77.2 %copy-start.13 = (bf16[192,384]{1,0:T(8,128)(2,1)S(1)}, bf16[192,384]{1,0:T(8,128)(2,1)}, u32[]{:S(2)}) copy-start(bf16[192,384]{1,0:T(8,128)(2,1)} %param.16) | copy-start | bytes 442372
  202.3 91.8 %all-to-all-start.2 = ((bf16[16,192,512]{2,1,0:T(8,128)(2,1)}), bf16[16,192,512]{2,1,0:T(8,128)(2,1)}, u32[]{:S(2)}, u32[]{:S(2)}) async-start(bf16[16,192,512]{2,1,0:T(8,128)(2,1)} %broadcast_in_dim.10), calls=%async_computation.2 | async-start | bytes 6291456 | tf_op jit(solution)/shard_map/all_to_all | solution.py:20
  208.1 199.8 %all-gather.14.cloned.1.call-start = ((), (), s32[]{:S(2)}) async-start(), calls=%async_computation.15 | async-start | bytes 2228224 | tf_op jit(solution)/shard_map/all_gather | solution.py:16
  290.3 2.8 copy-start.1
  298.5 0.7 copy-start.8
  298.8 1.0 copy-start.3
  301.9 26.5 %all-to-all-start.5 = ((bf16[16,192,128]{2,1,0:T(8,128)(2,1)}), bf16[16,192,128]{2,1,0:T(8,128)(2,1)}, u32[]{:S(2)}, u32[]{:S(2)}) async-start(bf16[16,192,128]{2,1,0:T(8,128)(2,1)} %broadcast_in_dim.12), calls=%async_computation.5 | async-start | bytes 1572864 | tf_op jit(solution)/shard_map/all_to_all | solution.py:20
  330.9 17.1 %all-to-all-start.6 = ((bf16[16,128,128]{2,1,0:T(8,128)(2,1)}), bf16[16,128,128]{2,1,0:T(8,128)(2,1)}, u32[]{:S(2)}, u32[]{:S(2)}) async-start(bf16[16,128,128]{2,1,0:T(8,128)(2,1)} %bitcast.120), calls=%async_computation.6 | async-start | bytes 1048576 | tf_op jit(solution)/shard_map/all_to_all | solution.py:24
  348.0 29.6 %all-to-all-start.1 = ((bf16[16,192,128]{2,1,0:T(8,128)(2,1)}), bf16[16,192,128]{2,1,0:T(8,128)(2,1)}, u32[]{:S(2)}, u32[]{:S(2)}) async-start(bf16[16,192,128]{2,1,0:T(8,128)(2,1)} %bitcast.114), calls=%async_computation.1 | async-start | bytes 1572864 | tf_op jit(solution)/shard_map/all_to_all | solution.py:73
  355.6 124.6 %all-gather.12.cloned.1.call-start = ((), (), s32[]{:S(2)}) async-start(), calls=%async_computation.14 | async-start | bytes 2228224 | tf_op jit(solution)/shard_map/all_gather | solution.py:16
  378.5 15.1 %all-to-all-start.7 = ((bf16[16,128,128]{2,1,0:T(8,128)(2,1)}), bf16[16,128,128]{2,1,0:T(8,128)(2,1)}, u32[]{:S(2)}, u32[]{:S(2)}) async-start(bf16[16,128,128]{2,1,0:T(8,128)(2,1)} %broadcast_in_dim.13), calls=%async_computation.7 | async-start | bytes 1048576 | tf_op jit(solution)/shard_map/all_to_all | solution.py:20
  384.8 19.3 %copy-start.7 = (bf16[128,512]{1,0:T(8,128)(2,1)S(1)}, bf16[128,512]{1,0:T(8,128)(2,1)}, u32[]{:S(2)}) copy-start(bf16[128,512]{1,0:T(8,128)(2,1)} %convolution_convert_fusion.7) | copy-start | bytes 393220
  393.6 29.5 %all-to-all-start.3 = ((bf16[16,192,128]{2,1,0:T(8,128)(2,1)}), bf16[16,192,128]{2,1,0:T(8,128)(2,1)}, u32[]{:S(2)}, u32[]{:S(2)}) async-start(bf16[16,192,128]{2,1,0:T(8,128)(2,1)} %bitcast.116), calls=%async_computation.3 | async-start | bytes 1572864 | tf_op jit(solution)/shard_map/all_to_all | solution.py:73
  407.9 4.7 copy-start.5
  412.7 14.8 %copy-start.9 = (bf16[512,384]{1,0:T(8,128)(2,1)S(1)}, bf16[512,384]{1,0:T(8,128)(2,1)}, u32[]{:S(2)}) copy-start(bf16[512,384]{1,0:T(8,128)(2,1)} %copy-done.8) | copy-start | bytes 1179652
  423.1 60.9 %all-to-all-start.9 = ((bf16[16,320,128]{2,1,0:T(8,128)(2,1)}), bf16[16,320,128]{2,1,0:T(8,128)(2,1)}, u32[]{:S(2)}, u32[]{:S(2)}) async-start(bf16[16,320,128]{2,1,0:T(8,128)(2,1)} %pad_maximum_fusion), calls=%async_computation.9 | async-start | bytes 2621440 | tf_op jit(solution)/shard_map/all_to_all | solution.py:24
  427.5 1.7 copy-start.4
  427.5 3.8 copy-start.14
  429.5 0.8 copy-start.6
  485.2 14.2 %all-to-all-start.4 = ((f32[16,1,128]{2,1,0:T(1,128)}), f32[16,1,128]{2,1,0:T(1,128)S(1)}, u32[]{:S(2)}, u32[]{:S(2)}) async-start(f32[16,1,128]{2,1,0:T(1,128)} %broadcast_in_dim_broadcast_in_dim_broadcast_in_dim.3), calls=%async_computation.4 | async-start | bytes 16384 | tf_op jit(solution)/shard_map/all_to_all | solution.py:20
  493.8 0.7 copy-start.10
  501.1 16.9 %all-to-all-start.10 = ((bf16[16,128,128]{2,1,0:T(8,128)(2,1)}), bf16[16,128,128]{2,1,0:T(8,128)(2,1)}, u32[]{:S(2)}, u32[]{:S(2)}) async-start(bf16[16,128,128]{2,1,0:T(8,128)(2,1)} %broadcast_in_dim.14), calls=%async_computation.10 | async-start | bytes 1048576 | tf_op jit(solution)/shard_map/all_to_all | solution.py:20
  518.0 35.2 %all-to-all-start.8 = ((bf16[16,192,384]{2,1,0:T(8,128)(2,1)}), bf16[16,192,384]{2,1,0:T(8,128)(2,1)}, u32[]{:S(2)}, u32[]{:S(2)}) async-start(bf16[16,192,384]{2,1,0:T(8,128)(2,1)} %bitcast.118), calls=%async_computation.8 | async-start | bytes 4718592 | tf_op jit(solution)/shard_map/all_to_all | solution.py:24
  522.4 4.5 copy-start.11
Sparse Core Ops, SparseCore 0:
  10.6 93.8 all-gather.5
  111.7 85.2 all-gather.7
  200.3 89.9 all-gather.9
  301.0 91.5 all-gather.13
  395.0 85.1 all-gather.11
